TPU v7x, 32 devices: a whole 2x2x4 slice. The times are simulated.
32 devices in a mesh: seq: 8 (over y, x, core), ch: 4 (over z).
Axes of the slice: x: 2, y: 2, z: 4, core: 2. Of those that a mesh axis runs over, the one named last changes fastest.
Arguments:
- tokens: bfloat16 [65536, 512], P('seq', 'ch'), may hold values from -6 to 6
- gate: bfloat16 [65536, 512], P('seq', 'ch'), may hold values from -6 to 6
- cotangent: bfloat16 [65536, 512], P('seq', 'ch'), may hold values from -6 to 6
- w_first: bfloat16 [1024, 1024], replicated, may hold values from -0.1875 to 0.1875
- w_second: bfloat16 [64, 64], replicated, may hold values from -0.75 to 0.75
Outputs:
- mixed: bfloat16 [65536, 512], P('seq', 'ch')
- grad_tokens: bfloat16 [65536, 512], P('seq', 'ch')
- grad_gate: bfloat16 [65536, 512], P('seq', 'ch')
- grad_first: float32 [1024, 1024], replicated
- grad_second: float32 [64, 64], replicated
All inputs are finite; a program needn't handle non-finite values.
Results may differ from a plain program's by a relative error of at most 0.0058.
Values may be sent and summed in bfloat16 or wider, within the bound.
A program may use at most 128 MiB of HBM per device.

v0:
```python
import jax
import jax.numpy as jnp
from jax import lax
from jax.sharding import PartitionSpec as P


def local(tokens, gate, cotangent, w_first, w_second):
    seq_count = lax.axis_size("seq")
    chan_count = lax.axis_size("ch")
    width = tokens.shape[1]
    block = w_first.shape[0]
    local_blocks = tokens.shape[0] // block
    all_blocks = local_blocks * seq_count
    x_blocks = tokens.reshape(local_blocks, block, width)
    gate_f = gate.reshape(local_blocks, block, width).astype(jnp.float32)
    cot_blocks = cotangent.reshape(local_blocks, block, width)
    first = jnp.einsum("jk,ikc->ijc", w_first, x_blocks, preferred_element_type=jnp.float32)
    sig = jax.nn.sigmoid(gate_f)
    act = gate_f * sig
    slope = sig * (1.0 + gate_f * (1.0 - sig))
    hidden = (first * act).astype(jnp.bfloat16)
    hidden_t = lax.all_to_all(hidden, "seq", split_axis=1, concat_axis=0, tiled=True)
    mixed_t = jnp.einsum(
        "il,ljc->ijc", w_second, hidden_t, preferred_element_type=jnp.float32
    ).astype(jnp.bfloat16)
    mixed = lax.all_to_all(mixed_t, "seq", split_axis=0, concat_axis=1, tiled=True)
    cot_t = lax.all_to_all(cot_blocks, "seq", split_axis=1, concat_axis=0, tiled=True)
    grad_hidden_t = jnp.einsum(
        "il,ijc->ljc", w_second, cot_t, preferred_element_type=jnp.float32
    ).astype(jnp.bfloat16)
    grad_hidden = lax.all_to_all(grad_hidden_t, "seq", split_axis=0, concat_axis=1, tiled=True)
    second_term = jnp.einsum("ijc,ljc->il", cot_t, hidden_t, preferred_element_type=jnp.float32)
    gh_float = grad_hidden.astype(jnp.float32)
    grad_first_act = (gh_float * act).astype(jnp.bfloat16)
    grad_gate = (gh_float * first * slope).astype(jnp.bfloat16)
    grad_tokens = jnp.einsum(
        "jk,ijc->ikc", w_first, grad_first_act, preferred_element_type=jnp.float32
    ).astype(jnp.bfloat16)
    first_term = jnp.einsum(
        "ijc,ikc->jk", grad_first_act, x_blocks, preferred_element_type=jnp.float32
    )
    first_sum, second_sum = lax.psum((first_term, second_term), ("seq", "ch"))
    total_width = width * chan_count
    grad_first = first_sum / jnp.sqrt(jnp.float32(all_blocks * total_width))
    grad_second = second_sum / jnp.sqrt(jnp.float32(block * total_width))
    rows = local_blocks * block
    return (
        mixed.reshape(rows, width),
        grad_tokens.reshape(rows, width),
        grad_gate.reshape(rows, width),
        grad_first,
        grad_second,
    )


def solution(mesh):
    return jax.shard_map(
        local,
        mesh=mesh,
        in_specs=(P("seq", "ch"), P("seq", "ch"), P("seq", "ch"), P(), P()),
        out_specs=(P("seq", "ch"), P("seq", "ch"), P("seq", "ch"), P(), P()),
        check_vma=False,
    )
```

profile of v0, /device:TPU:0, one launch (start us, length us, event | category | flops | bytes accessed | tf_op | source)
XLA Modules:
  0.0 284.2 jit_solution(8243731049604911100)
XLA Ops:
  7.2 0.0 copy-start
  7.2 3.1 %copy.58 = bf16[8,1024,128]{2,0,1:T(8,128)(2,1)S(1)} copy(bf16[8,1024,128]{2,1,0:T(8,128)(2,1)} %bitcast.85) | data formatting | bytes 4194304 | tf_op jit(solution)/shard_map/reshape | solution.py:16
  10.3 0.0 copy-start.5
  10.3 31.6 %all_to_all.60 = bf16[8,1024,128]{2,0,1:T(8,128)(2,1)S(1)} all-to-all(bf16[8,1024,128]{2,0,1:T(8,128)(2,1)S(1)} %copy.58), channel_id=1, replica_groups=mesh['seq'=8,'ch'=4] {'seq'}, dimensions={1} | all-to-all | bytes 4194304 | tf_op jit(solution)/shard_map/all_to_all | solution.py:27
  41.9 1.4 copy-done.2
  43.2 0.7 fusion.17
  44.0 2.7 copy.62
  46.6 4.3 %all-to-all-start.3 = ((bf16[64,128,128]{2,1,0:T(8,128)(2,1)}), bf16[64,128,128]{2,1,0:T(8,128)(2,1)}, u32[]{:S(2)}, u32[]{:S(2)}) async-start(bf16[64,128,128]{2,1,0:T(8,128)(2,1)} %copy.62), calls=%async_computation.3 | async-start | bytes 4194304 | tf_op jit(solution)/shard_map/all_to_all | solution.py:31
  51.0 4.1 %copy.53 = f32[8,1024,128]{1,2,0:T(8,128)} copy(bf16[8,1024,128]{2,1,0:T(8,128)(2,1)} %bitcast.84) | data formatting | bytes 6291456 | tf_op jit(solution)/shard_map/convert_element_type | solution.py:15
  55.1 22.5 %all-to-all-done.3 = bf16[64,128,128]{2,1,0:T(8,128)(2,1)} async-done(((bf16[64,128,128]{2,1,0:T(8,128)(2,1)}), bf16[64,128,128]{2,1,0:T(8,128)(2,1)}, u32[]{:S(2)}, u32[]{:S(2)}) %all-to-all-start.3) | async-done | bytes 2097184 | tf_op jit(solution)/shard_map/all_to_all | solution.py:31
  77.6 4.1 %copy.63 = f32[8,8,128,128]{2,0,3,1:T(8,128)} copy(bf16[8,8,128,128]{3,2,1,0:T(8,128)(2,1)} %bitcast.29) | data formatting | bytes 6291456 | tf_op jit(solution)/shard_map/convert_element_type | solution.py:33
  81.8 4.9 %reshape.39 = f32[8,1024,128]{1,2,0:T(8,128)} reshape(f32[8,8,128,128]{2,1,3,0:T(8,128)} %bitcast.81) | data formatting | bytes 8388608 | tf_op jit(solution)/shard_map/convert_element_type | solution.py:33
  86.7 8.7 %fusion.2 = (bf16[8,1024,128]{1,2,0:T(8,128)(2,1)}, bf16[8,1024,128]{1,2,0:T(8,128)(2,1)}, bf16[8,1024,128]{1,2,0:T(8,128)(2,1)}) fusion(f32[8,1024,128]{1,2,0:T(8,128)} %reshape.39, f32[8,1024,128]{1,2,0:T(8,128)} %copy.53, bf16[8,1024,128]{2,1,0:T(8,128)(2,1)S(1)} %bitcast.79, bf16[1024,1024]{1,0:T(8,128)(2,1)} %param.8), kind=kOutput, calls=%fused_computation.4 | convolution fusion | flops 2163212288 | bytes 18874368 | tf_op jit(solution)/shard_map/jk,ikc->ijc/dot_general | solution.py:17
  95.3 4.2 %copy.54 = bf16[8,1024,128]{2,0,1:T(8,128)(2,1)} copy(bf16[8,1024,128]{1,2,0:T(8,128)(2,1)} %get-tuple-element.26) | data formatting | bytes 4194304 | tf_op jit(solution)/shard_map/convert_element_type | solution.py:21
  99.6 4.3 %all-to-all-start = ((bf16[8,1024,128]{2,0,1:T(8,128)(2,1)}), bf16[8,1024,128]{2,0,1:T(8,128)(2,1)}, u32[]{:S(2)}, u32[]{:S(2)}) async-start(bf16[8,1024,128]{2,0,1:T(8,128)(2,1)} %copy.54), calls=%async_computation | async-start | bytes 4194304 | tf_op jit(solution)/shard_map/all_to_all | solution.py:22
  103.9 0.2 all-reduce.2.cloned.1.call-start
  104.1 6.0 %convolution_bitcast_fusion = f32[1024,1024]{1,0:T(8,128)} fusion(bf16[8,1024,128]{1,2,0:T(8,128)(2,1)} %get-tuple-element.27, bf16[8,1024,128]{2,1,0:T(8,128)(2,1)S(1)} %bitcast.80), kind=kOutput, calls=%fused_computation.8 | convolution fusion | flops 2147483648 | bytes 8388608 | tf_op jit(solution)/shard_map/ijc,ikc->jk/dot_general | solution.py:39
  110.1 0.0 all-reduce.2.cloned.1.call-update
  110.2 26.1 %all-to-all-done = bf16[8,1024,128]{2,0,1:T(8,128)(2,1)} async-done(((bf16[8,1024,128]{2,0,1:T(8,128)(2,1)}), bf16[8,1024,128]{2,0,1:T(8,128)(2,1)}, u32[]{:S(2)}, u32[]{:S(2)}) %all-to-all-start) | async-done | bytes 2097184 | tf_op jit(solution)/shard_map/all_to_all | solution.py:22
  136.2 2.3 convert_bitcast_fusion.1
  138.6 2.7 copy.56
  141.2 4.5 %all-to-all-start.1 = ((bf16[64,128,128]{2,1,0:T(8,128)(2,1)}), bf16[64,128,128]{2,1,0:T(8,128)(2,1)}, u32[]{:S(2)}, u32[]{:S(2)}) async-start(bf16[64,128,128]{2,1,0:T(8,128)(2,1)} %copy.56), calls=%async_computation.1 | async-start | bytes 4194304 | tf_op jit(solution)/shard_map/all_to_all | solution.py:26
  145.7 2.4 copy.66
  148.1 5.9 %convert_bitcast_fusion = bf16[8,1024,128]{1,2,0:T(8,128)(2,1)} fusion(bf16[8,1024,128]{1,2,0:T(8,128)(2,1)} %get-tuple-element.27, bf16[1024,1024]{1,0:T(8,128)(2,1)} %param.8), kind=kOutput, calls=%fused_computation.21 | convolution fusion | flops 2148532224 | bytes 6291456 | tf_op jit(solution)/shard_map/jk,ijc->ikc/dot_general | solution.py:36
  154.1 4.1 %copy.64 = bf16[8,1024,128]{2,1,0:T(8,128)(2,1)} copy(bf16[8,1024,128]{1,2,0:T(8,128)(2,1)} %convert_bitcast_fusion) | data formatting | bytes 4194304 | tf_op jit(solution)/shard_map/convert_element_type | solution.py:38
  158.1 2.3 fusion.26
  160.4 48.6 %psum.15 = f32[64,64]{0,1:T(8,128)S(1)} all-reduce(f32[64,64]{0,1:T(8,128)S(1)} %fusion.26), channel_id=1, replica_groups=mesh['seq'=8,'ch'=4] {'seq','ch'}, use_global_device_ids=true, to_apply=%region_1.0 | all-reduce | flops 4096 | bytes 32768 | tf_op jit(solution)/shard_map/psum | solution.py:42
  209.1 0.7 copy.68
  209.8 59.1 %all-reduce.2.cloned.1.call-done = f32[1024,1024]{1,0:T(8,128)} async-done(((f32[1024,1024]{1,0:T(8,128)}), f32[1024,1024]{1,0:T(8,128)}) %all-reduce.2.cloned.1.call-update) | async-done | bytes 4194320 | tf_op jit(solution)/shard_map/psum | solution.py:42
  268.9 5.1 %broadcast_multiply_fusion = f32[1024,1024]{1,0:T(8,128)} fusion(f32[1024,1024]{1,0:T(8,128)} %all-reduce.2.cloned.1.call-done), kind=kLoop, calls=%fused_computation.20 | loop fusion | flops 1048576 | bytes 8388608 | tf_op jit(solution)/shard_map/div | solution.py:44
  274.0 0.0 all-to-all-done.1
  274.0 3.3 %copy.57 = bf16[8,8,128,128]{3,2,1,0:T(8,128)(2,1)} copy(bf16[8,8,128,128]{3,2,0,1:T(8,128)(2,1)} %bitcast.11) | data formatting | bytes 4194304 | tf_op jit(solution)/shard_map/all_to_all | solution.py:26
  (10 shorter events, 0.0 us)
Async XLA Ops:
  7.2 79.5 %copy-start = (bf16[8192,128]{1,0:T(8,128)(2,1)S(1)}, bf16[8192,128]{1,0:T(8,128)(2,1)}, u32[]{:S(2)}) copy-start(bf16[8192,128]{1,0:T(8,128)(2,1)} %param.5) | copy-start | bytes 6291460
  10.3 32.9 %copy-start.5 = (bf16[64,64]{1,0:T(8,128)(2,1)S(1)}, bf16[64,64]{1,0:T(8,128)(2,1)}, u32[]{:S(2)}) copy-start(bf16[64,64]{1,0:T(8,128)(2,1)} %param.9) | copy-start | bytes 24580
  41.9 1.4 copy-start.2
  46.6 31.0 %all-to-all-start.3 = ((bf16[64,128,128]{2,1,0:T(8,128)(2,1)}), bf16[64,128,128]{2,1,0:T(8,128)(2,1)}, u32[]{:S(2)}, u32[]{:S(2)}) async-start(bf16[64,128,128]{2,1,0:T(8,128)(2,1)} %copy.62), calls=%async_computation.3 | async-start | bytes 4194304 | tf_op jit(solution)/shard_map/all_to_all | solution.py:31
  99.6 36.7 %all-to-all-start = ((bf16[8,1024,128]{2,0,1:T(8,128)(2,1)}), bf16[8,1024,128]{2,0,1:T(8,128)(2,1)}, u32[]{:S(2)}, u32[]{:S(2)}) async-start(bf16[8,1024,128]{2,0,1:T(8,128)(2,1)} %copy.54), calls=%async_computation | async-start | bytes 4194304 | tf_op jit(solution)/shard_map/all_to_all | solution.py:22
  103.9 165.0 %all-reduce.2.cloned.1.call-start = ((), (), s32[]{:S(2)}) async-start(), calls=%async_computation.4 | async-start | bytes 8388608 | tf_op jit(solution)/shard_map/psum | solution.py:42
  141.2 4.5 %copy-start.4 = (bf16[8,1024,128]{1,2,0:T(8,128)(2,1)S(1)}, bf16[8,1024,128]{1,2,0:T(8,128)(2,1)}, u32[]{:S(2)}) copy-start(bf16[8,1024,128]{1,2,0:T(8,128)(2,1)} %get-tuple-element.25) | copy-start | bytes 6291460
  141.2 132.8 %all-to-all-start.1 = ((bf16[64,128,128]{2,1,0:T(8,128)(2,1)}), bf16[64,128,128]{2,1,0:T(8,128)(2,1)}, u32[]{:S(2)}, u32[]{:S(2)}) async-start(bf16[64,128,128]{2,1,0:T(8,128)(2,1)} %copy.56), calls=%async_computation.1 | async-start | bytes 4194304 | tf_op jit(solution)/shard_map/all_to_all | solution.py:26
  154.1 4.1 %copy-start.3 = (bf16[8,1024,128]{2,0,1:T(8,128)(2,1)S(1)}, bf16[8,1024,128]{2,0,1:T(8,128)(2,1)}, u32[]{:S(2)}) copy-start(bf16[8,1024,128]{2,0,1:T(8,128)(2,1)} %copy-done.2) | copy-start | bytes 6291460
  274.0 3.3 %copy-start.1 = (bf16[8192,128]{1,0:T(8,128)(2,1)S(1)}, bf16[8192,128]{1,0:T(8,128)(2,1)}, u32[]{:S(2)}) copy-start(bf16[8192,128]{1,0:T(8,128)(2,1)} %param.5) | copy-start | bytes 6291460
Sparse Core Ops, SparseCore 0:
  110.9 157.9 all-reduce.1
where the time goes:
time: 285 us; the launch traced here: 284 us
  waiting for transfers between devices  108 us (38%)
  blocking collectives  80.2 us (28%)
  local copies, waits for them, and re-layouts  37.6 us (13%)
  matrix products  25.9 us (9%)
  between operations  14.1 us (5%)
  starting transfers between devices  13.4 us (5%)
  other arithmetic  5.13 us (2%)
    psum x1, waiting for transfers between devices, local(): first_sum, second_sum = lax.psum((first_term, second_term), ('seq', 'ch'))  59.1 us
    psum x1, blocking collectives, local(): first_sum, second_sum = lax.psum((first_term, second_term), ('seq', 'ch'))  48.6 us
    all_to_all x1, blocking collectives, local(): lax.all_to_all(cot_blocks, 'seq', split_axis=1, concat_axis=0, tiled=True)  31.6 us
    all_to_all x1, waiting for transfers between devices, local(): lax.all_to_all(hidden, 'seq', split_axis=1, concat_axis=0, tiled=True)  26.1 us
    all_to_all x1, waiting for transfers between devices, local(): lax.all_to_all(grad_hidden_t, 'seq', split_axis=0, concat_axis=1, tiled=T...  22.5 us
    convert_element_type x2, local copies, waits for them, and re-layouts, local(): gh_float = grad_hidden.astype(jnp.float32)  9.05 us
    dot_general x1, matrix products, local(): jnp.einsum('jk,ikc->ijc', w_first, x_blocks, preferred_element_type=jnp.f...  8.67 us
    dot_general x1, matrix products, local(): jnp.einsum('ijc,ikc->jk', grad_first_act, x_blocks, preferred_element_typ...  5.99 us
  transfers between devices with their start and end apart: 4, of which 3 were waited for; matrix products, arithmetic and copies ran while one was open for 13% of the time, Pallas kernels for 0%

commit v1 on v0

--- a/solution.py
+++ b/solution.py
@@ -1,7 +1,414 @@
+import functools
+
 import jax
 import jax.numpy as jnp
 from jax import lax
+from jax.experimental import pallas as pl
+from jax.experimental.pallas import tpu as pltpu
 from jax.sharding import PartitionSpec as P
+
+MESH = pl.DeviceIdType.MESH
+BF = jnp.bfloat16
+F32 = jnp.float32
+GRP = 16
+CHUNKS = 2
+NT = (((1,), (1,)), ((), ()))
+TN = (((0,), (0,)), ((), ()))
+
+
+def dot(a, b, dims=(((1,), (0,)), ((), ()))):
+    return lax.dot_general(a, b, dims, preferred_element_type=F32)
+
+
+def loop(lo, hi, body):
+    def step(i, carry):
+        body(i)
+        return carry
+
+    lax.fori_loop(lo, hi, step, 0)
+
+
+def remote(src, dst, send, recv, dev):
+    return pltpu.make_async_remote_copy(
+        src_ref=src, dst_ref=dst, send_sem=send, recv_sem=recv, device_id=dev, device_id_type=MESH
+    )
+
+
+def fused(ns, nch, lb, pp, width,
+          x_hbm, g_hbm, dz_hbm, w1_hbm, w2_ref,
+          mixed_hbm, gt_hbm, gg_hbm, gf_hbm, gs_ref,
+          xv, gv, w1v, wk, wkt, act, fs, hid, dzt, ht, ght, ghr, mt, gfa, gtv,
+          pf, pb, r1, s1b, r2, s2, s2b, r3, gfo, gsr, gsr2,
+          ld, dz_l, mx_l, out_l,
+          dz_s, dz_r, gh_s, gh_r, h_s, h_r, mx_s, mx_r,
+          a1_s, a1_r, a2_s, a2_r, a3_s, a3_r, b3_s, b3_r, b2_s, b2_r, b1_s, b1_r,
+          q_s, q_r, q2_s, q2_r):
+    nc = CHUNKS
+    pc = pp // nc
+    block = ns * pp
+    nb = lb * ns
+    big = nb * GRP
+    me = lax.axis_index("seq")
+    zz = lax.axis_index("ch")
+    core = lax.rem(me, 2)
+    quad = me // 2
+    nq = ns // 2
+    half = block // nc // 2
+    zrows = half // nch
+    qrows = zrows // nq
+
+    def peer(d):
+        return lax.rem(me + d, ns)
+
+    def zpeer(d):
+        return lax.rem(zz + d, nch)
+
+    def qpeer(d):
+        return lax.rem(quad + d, nq)
+
+    loads = [
+        pltpu.make_async_copy(w1_hbm, w1v, ld.at[0]),
+        pltpu.make_async_copy(x_hbm, xv, ld.at[1]),
+        pltpu.make_async_copy(g_hbm, gv, ld.at[2]),
+    ]
+    dz_own = [
+        pltpu.make_async_copy(dz_hbm.at[:, me, h], dzt.at[h, pl.ds(me * lb, lb)], dz_l.at[h])
+        for h in range(nc)
+    ]
+    for c in loads:
+        c.start()
+    for c in dz_own:
+        c.start()
+
+    barrier = pltpu.get_barrier_semaphore()
+    loop(1, ns, lambda d: pl.semaphore_signal(barrier, inc=1, device_id={"seq": peer(d)}, device_id_type=MESH))
+    loop(1, nch, lambda d: pl.semaphore_signal(barrier, inc=1, device_id={"ch": zpeer(d)}, device_id_type=MESH))
+    pl.semaphore_wait(barrier, ns + nch - 2)
+
+    mine = pl.ds(me * lb, lb)
+
+    def dz_copy(h, d):
+        return remote(dz_hbm.at[:, peer(d), h], dzt.at[h, mine], dz_s.at[h, d], dz_r.at[h, d], {"seq": peer(d)})
+
+    def gh_copy(h, d):
+        return remote(ght.at[h, pl.ds(peer(d) * lb, lb)], ghr.at[h, me], gh_s.at[h, d], gh_r.at[h, d], {"seq": peer(d)})
+
+    def h_copy(h, d):
+        return remote(hid.at[:, peer(d), h], ht.at[h, mine], h_s.at[h, d], h_r.at[h, d], {"seq": peer(d)})
+
+    def mx_copy(h, d):
+        return remote(mt.at[h, pl.ds(peer(d) * lb, lb)], mixed_hbm.at[:, me, h], mx_s.at[h, d], mx_r.at[h, d], {"seq": peer(d)})
+
+    def start(f, h, n):
+        loop(1, n, lambda d: f(h, d).start())
+
+    def recv(f, h, n):
+        loop(1, n, lambda d: f(h, d).wait_recv())
+
+    def sent(f, h, n):
+        loop(1, n, lambda d: f(h, d).wait_send())
+
+    for h in range(nc):
+        start(dz_copy, h, ns)
+
+    tile = 256
+
+    def onehot(rows, cols, first_row):
+        r = lax.broadcasted_iota(jnp.int32, (rows, cols), 0) + first_row
+        c = lax.broadcasted_iota(jnp.int32, (rows, cols), 1)
+        return jnp.where(r // GRP == c, 1.0, 0.0).astype(F32)
+
+    def same(rows, cols):
+        r = lax.broadcasted_iota(jnp.int32, (rows, cols), 0)
+        c = lax.broadcasted_iota(jnp.int32, (rows, cols), 1)
+        return r % GRP == c % GRP
+
+    def expand(t):
+        rows = pl.ds(pl.multiple_of(t * tile, tile), tile)
+        e = onehot(tile, nb, t * tile).astype(BF)
+        every = onehot(big, nb, 0).astype(BF)
+        keep = same(tile, big)
+        w2 = w2_ref[...]
+        wk[rows, :] = jnp.where(keep, dot(dot(e, w2).astype(BF), every, NT), 0.0).astype(BF)
+        wkt[rows, :] = jnp.where(keep, dot(dot(e, w2, NT).astype(BF), every, NT), 0.0).astype(BF)
+
+    loop(0, big // tile, expand)
+
+    for c in loads:
+        c.wait()
+
+    def forward(i):
+        b = jnp.concatenate(
+            [xv[2 * i].reshape(block, width), xv[2 * i + 1].reshape(block, width)], axis=1
+        )
+        f2 = dot(w1v[...], b)
+        for s in range(2):
+            f = f2[:, s * width : (s + 1) * width]
+            g = gv[2 * i + s].reshape(block, width).astype(F32)
+            sig = 1.0 / (1.0 + jnp.exp(-g))
+            a = g * sig
+            shape = (ns, nc, pc, width)
+            act[2 * i + s] = a.reshape(shape)
+            fs[2 * i + s] = (f * (sig * (1.0 + g * (1.0 - sig)))).reshape(shape)
+            hid[2 * i + s] = (f * a).astype(BF).reshape(shape)
+
+    loop(0, lb // 2, forward)
+
+    def pair(ref, h, q, rows):
+        lo = pl.multiple_of(q * 2 * GRP, 2 * GRP)
+        hi = pl.multiple_of(lo + GRP, GRP)
+        n = rows.size * GRP
+        return jnp.concatenate(
+            [ref[h, rows, pl.ds(lo, GRP), :].reshape(n, width), ref[h, rows, pl.ds(hi, GRP), :].reshape(n, width)],
+            axis=1,
+        )
+
+    def mix(w_ref, src, dst, h):
+        def body(q):
+            lo = pl.multiple_of(q * 2 * GRP, 2 * GRP)
+            hi = pl.multiple_of(lo + GRP, GRP)
+            out = dot(w_ref[...], pair(src, h, q, pl.ds(0, nb))).astype(BF)
+            dst[h, :, pl.ds(lo, GRP), :] = out[:, :width].reshape(nb, GRP, width)
+            dst[h, :, pl.ds(hi, GRP), :] = out[:, width:].reshape(nb, GRP, width)
+
+        loop(0, pc // (2 * GRP), body)
+
+    for h in range(nc):
+        dz_own[h].wait()
+        recv(dz_copy, h, ns)
+        mix(wkt, dzt, ght, h)
+        start(gh_copy, h, ns)
+        ghr[h, me] = ght[h, mine]
+
+    def a1(h):
+        return remote(pb.at[h, pl.ds((1 - core) * half, half)], r1.at[h], a1_s.at[h], a1_r.at[h], {"seq": me + 1 - 2 * core})
+
+    def a2(h, d):
+        return remote(s1b.at[h, pl.ds(zpeer(d) * zrows, zrows)], r2.at[h, d], a2_s.at[h, d], a2_r.at[h, d], {"ch": zpeer(d)})
+
+    def a3(h, d):
+        return remote(s2b.at[h, pl.ds(qpeer(d) * qrows, qrows)], r3.at[h, d], a3_s.at[h, d], a3_r.at[h, d], {"seq": qpeer(d) * 2 + core})
+
+    def b3(h, d):
+        part = gfo.at[h, pl.ds(core * half + zz * zrows + quad * qrows, qrows)]
+        return remote(part, part, b3_s.at[h, d], b3_r.at[h, d], {"seq": qpeer(d) * 2 + core})
+
+    def b2(h, d):
+        part = gfo.at[h, pl.ds(core * half + zz * zrows, zrows)]
+        return remote(part, part, b2_s.at[h, d], b2_r.at[h, d], {"ch": zpeer(d)})
+
+    def b1(h):
+        part = gfo.at[h, pl.ds(core * half, half)]
+        return remote(part, part, b1_s.at[h], b1_r.at[h], {"seq": me + 1 - 2 * core})
+
+    per = tile // pp
+
+    def term(h):
+        def gates(p):
+            gh = ghr[h, p].astype(F32)
+            gfa[:, p, h] = (gh * act[:, p, h]).astype(BF)
+            gv[:, p, h] = (gh * fs[:, p, h]).astype(BF)
+
+        loop(0, ns, gates)
+
+        def cols(t):
+            acc = None
+            for i in range(0, lb, 2):
+                a = jnp.concatenate(
+                    [gfa[i + s, :, h].reshape(ns * pc, width) for s in range(2)], axis=1
+                )
+                b = jnp.concatenate(
+                    [xv[i + s, pl.ds(t * per, per)].reshape(tile, width) for s in range(2)], axis=1
+                )
+                v = dot(a, b, NT)
+                acc = v if acc is None else acc + v
+            where = pl.ds(pl.multiple_of(t * tile, tile), tile)
+            pf[h, :, where] = acc
+            pb[h, :, where] = acc.astype(BF)
+
+        loop(0, block // tile, cols)
+
+    for h in range(nc):
+        recv(gh_copy, h, ns)
+        start(h_copy, h, ns)
+        ht[h, mine] = hid[:, me, h]
+        term(h)
+        a1(h).start()
+
+    for h in range(nc):
+        a1(h).wait_recv()
+        low = pl.ds(pl.multiple_of(core * half, half), half)
+        total = pf[h, low, :] + r1[h].astype(F32)
+        pf[h, low, :] = total
+        s1b[h] = total.astype(BF)
+        start(a2, h, nch)
+
+    out_gg = pltpu.make_async_copy(gv, gg_hbm, out_l.at[0])
+    out_gg.start()
+
+    def tokens(i):
+        b = jnp.concatenate(
+            [gfa[2 * i].reshape(block, width), gfa[2 * i + 1].reshape(block, width)], axis=1
+        )
+        out = dot(w1v[...], b, TN).astype(BF)
+        for s in range(2):
+            gtv[2 * i + s] = out[:, s * width : (s + 1) * width].reshape(ns, nc, pc, width)
+
+    loop(0, lb // 2, tokens)
+    out_gt = pltpu.make_async_copy(gtv, gt_hbm, out_l.at[1])
+    out_gt.start()
+
+    mx_own = [
+        pltpu.make_async_copy(mt.at[h, mine], mixed_hbm.at[:, me, h], mx_l.at[h]) for h in range(nc)
+    ]
+    for h in range(nc):
+        recv(h_copy, h, ns)
+        mix(wk, ht, mt, h)
+        start(mx_copy, h, ns)
+        mx_own[h].start()
+
+    for h in range(nc):
+        recv(a2, h, nch)
+        low = pl.multiple_of(core * half + zz * zrows, zrows)
+        total = pf[h, pl.ds(low, zrows), :]
+        for d in range(1, nch):
+            total = total + r2[h, d].astype(F32)
+        s2[h] = total
+        s2b[h] = total.astype(BF)
+        start(a3, h, nq)
+
+    def second(t):
+        rows = pl.ds(t * (tile // GRP), tile // GRP)
+        acc = None
+        for h in range(nc):
+            for q in range(pc // (2 * GRP)):
+                v = dot(pair(dzt, h, q, rows), pair(ht, h, q, pl.ds(0, nb)), NT)
+                acc = v if acc is None else acc + v
+        acc = jnp.where(same(tile, big), acc, 0.0)
+        acc = acc.reshape(tile // GRP, GRP, big).sum(axis=1)
+        gsr[me, pl.ds(pl.multiple_of(t * (tile // GRP), tile // GRP), tile // GRP), :] = lax.dot_general(
+            acc, onehot(big, 128, 0), (((1,), (0,)), ((), ())),
+            precision=lax.Precision.HIGHEST, preferred_element_type=F32,
+        )
+
+    loop(0, big // tile, second)
+
+    def q1(h, d):
+        return remote(gsr.at[me], gsr.at[me], q_s.at[d], q_r.at[d], {"seq": peer(d)})
+
+    def q2(h, d):
+        return remote(gsr2.at[zz], gsr2.at[zz], q2_s.at[d], q2_r.at[d], {"ch": zpeer(d)})
+
+    start(q1, 0, ns)
+
+    for h in range(nc):
+        recv(a3, h, nq)
+        total = s2[h, pl.ds(pl.multiple_of(quad * qrows, qrows), qrows), :]
+        for d in range(1, nq):
+            total = total + r3[h, d].astype(F32)
+        gfo[h, pl.ds(pl.multiple_of(core * half + zz * zrows + quad * qrows, qrows), qrows), :] = total.astype(BF)
+        start(b3, h, nq)
+
+    for h in range(nc):
+        recv(b3, h, nq)
+        sent(b3, h, nq)
+        start(b2, h, nch)
+
+    recv(q1, 0, ns)
+    sent(q1, 0, ns)
+    total = gsr[0]
+    for d in range(1, ns):
+        total = total + gsr[d]
+    gsr2[zz] = total
+    start(q2, 0, nch)
+
+    for h in range(nc):
+        recv(b2, h, nch)
+        sent(b2, h, nch)
+        b1(h).start()
+
+    recv(q2, 0, nch)
+    sent(q2, 0, nch)
+    total = gsr2[0]
+    for d in range(1, nch):
+        total = total + gsr2[d]
+    gs_ref[...] = total
+
+    for h in range(nc):
+        b1(h).wait_recv()
+        b1(h).wait_send()
+    out_gf = pltpu.make_async_copy(gfo, gf_hbm, out_l.at[2])
+    out_gf.start()
+
+    for h in range(nc):
+        sent(dz_copy, h, ns)
+        sent(gh_copy, h, ns)
+        sent(h_copy, h, ns)
+        a1(h).wait_send()
+        sent(a2, h, nch)
+        sent(a3, h, nq)
+    for h in range(nc):
+        mx_own[h].wait()
+        recv(mx_copy, h, ns)
+        sent(mx_copy, h, ns)
+    out_gg.wait()
+    out_gt.wait()
+    out_gf.wait()
+
+
+def local_fused(tokens, gate, cotangent, w_first, w_second):
+    ns = lax.axis_size("seq")
+    nch = lax.axis_size("ch")
+    width = tokens.shape[1]
+    block = w_first.shape[0]
+    lb = tokens.shape[0] // block
+    nb = lb * ns
+    pp = block // ns
+    nc = CHUNKS
+    pc = pp // nc
+    nq = ns // 2
+    half = block // nc // 2
+    zrows = half // nch
+    qrows = zrows // nq
+    big = nb * GRP
+    five = (lb, ns, nc, pc, width)
+    spread = (nc, nb, pc, width)
+    anyspec = pl.BlockSpec(memory_space=pl.ANY)
+    vmem = pl.BlockSpec(memory_space=pltpu.VMEM)
+    V = pltpu.VMEM
+    D = pltpu.SemaphoreType.DMA
+    scratch = [
+        V(five, BF), V(five, BF), V((block, block), BF), V((big, big), BF), V((big, big), BF),
+        V(five, F32), V(five, F32), V(five, BF),
+        V(spread, BF), V(spread, BF), V(spread, BF), V((nc, ns, lb, pc, width), BF), V(spread, BF),
+        V(five, BF), V(five, BF),
+        V((nc, 2 * half, block), F32), V((nc, 2 * half, block), BF),
+        V((nc, half, block), BF), V((nc, half, block), BF),
+        V((nc, nch, zrows, block), BF), V((nc, zrows, block), F32), V((nc, zrows, block), BF),
+        V((nc, nq, qrows, block), BF), V((nc, 2 * half, block), BF),
+        V((ns, nb, 128), F32), V((nch, nb, 128), F32),
+        D((3,)), D((nc,)), D((nc,)), D((3,)),
+    ]
+    scratch += [D((nc, ns))] * 8
+    scratch += [D((nc,))] * 2 + [D((nc, nch))] * 2 + [D((nc, nq))] * 4 + [D((nc, nch))] * 2 + [D((nc,))] * 2
+    scratch += [D((ns,))] * 2 + [D((nch,))] * 2
+    sd = jax.ShapeDtypeStruct
+    mixed, gt, gg, gf, gs = pl.pallas_call(
+        functools.partial(fused, ns, nch, lb, pp, width),
+        out_shape=(sd(five, BF), sd(five, BF), sd(five, BF), sd((nc, 2 * half, block), BF), sd((nb, 128), F32)),
+        in_specs=[anyspec] * 4 + [vmem],
+        out_specs=(anyspec, anyspec, anyspec, anyspec, vmem),
+        scratch_shapes=scratch,
+        compiler_params=pltpu.CompilerParams(
+            collective_id=0, has_side_effects=True, vmem_limit_bytes=60 * 1024 * 1024
+        ),
+        name="fused",
+    )(tokens.reshape(five), gate.reshape(five), cotangent.reshape(five), w_first, w_second)
+    total_width = width * nch
+    gf = gf.reshape(nc, ns, pc, block).transpose(1, 0, 2, 3).reshape(block, block)
+    grad_first = gf.astype(F32) / jnp.sqrt(F32(nb * total_width))
+    grad_second = gs[:, :nb] / jnp.sqrt(F32(block * total_width))
+    return mixed.reshape(tokens.shape), gt.reshape(tokens.shape), gg.reshape(tokens.shape), grad_first, grad_second
 
 
 def local(tokens, gate, cotangent, w_first, w_second):
@@ -53,11 +460,27 @@
     )
 
 
+def fits(mesh, tokens, w_first):
+    ns, nch = mesh.shape["seq"], mesh.shape["ch"]
+    block = w_first.shape[0]
+    width = tokens.shape[1] // nch
+    lb = tokens.shape[0] // ns // block
+    pp = block // ns
+    if width != 128 or lb % 2 or ns % 2 or lb * ns * GRP > 1024 or (lb * ns * GRP) % 256:
+        return False
+    if block > 1024 or block % 256 or 256 % pp or pp % (CHUNKS * 2 * GRP):
+        return False
+    return (block // CHUNKS) % (ns * nch * GRP) == 0 and lb * ns <= 128 and lb <= 8
+
+
 def solution(mesh):
-    return jax.shard_map(
-        local,
-        mesh=mesh,
-        in_specs=(P("seq", "ch"), P("seq", "ch"), P("seq", "ch"), P(), P()),
-        out_specs=(P("seq", "ch"), P("seq", "ch"), P("seq", "ch"), P(), P()),
-        check_vma=False,
-    )
+    def run(tokens, gate, cotangent, w_first, w_second):
+        return jax.shard_map(
+            local_fused if fits(mesh, tokens, w_first) else local,
+            mesh=mesh,
+            in_specs=(P("seq", "ch"), P("seq", "ch"), P("seq", "ch"), P(), P()),
+            out_specs=(P("seq", "ch"), P("seq", "ch"), P("seq", "ch"), P(), P()),
+            check_vma=False,
+        )(tokens, gate, cotangent, w_first, w_second)
+
+    return run

time: 285 us -> 149 us (0.52)
  Pallas kernels: 0 us -> 136 us
  waiting for transfers between devices: 108 us -> 0 us
  blocking collectives: 80.2 us -> 0 us
  local copies, waits for them, and re-layouts: 37.6 us -> 8.34 us
  matrix products: 25.9 us -> 0 us
  between operations: 14.1 us -> 0.66 us
  starting transfers between devices: 13.4 us -> 0 us
    pallas_call x0 -> x1, Pallas kernels: none -> 136 us  [local_fused(): pl.pallas_call(functools.partial(fused, ns, nch, lb, pp, width), out_shap...]
    psum x1 -> x0, waiting for transfers between devices: 59.1 us -> none  [local(): first_sum, second_sum = lax.psum((first_term, second_term), ('seq', 'ch'))]
    psum x1 -> x0, blocking collectives: 48.6 us -> none  [local(): first_sum, second_sum = lax.psum((first_term, second_term), ('seq', 'ch'))]
    all_to_all x3 -> x0, waiting for transfers between devices: 48.6 us -> none  [the longest x1 26.1 us: local(): lax.all_to_all(hidden, 'seq', split_axis=1, concat_axis=0, tiled=True)]
    all_to_all x1 -> x0, blocking collectives: 31.6 us -> none  [local(): lax.all_to_all(cot_blocks, 'seq', split_axis=1, concat_axis=0, tiled=True)]
    convert_element_type x8 -> x0, local copies, waits for them, and re-layouts: 29.2 us -> none  [the longest x2 9.05 us: local(): gh_float = grad_hidden.astype(jnp.float32)]
    dot_general x6 -> x0, matrix products: 25.9 us -> none  [the longest x1 8.67 us: local(): jnp.einsum('jk,ikc->ijc', w_first, x_blocks, preferred_element_type=jnp.f...]
    all_to_all x3 -> x0, starting transfers between devices: 13.2 us -> none  [the longest x1 4.48 us: local(): lax.all_to_all(mixed_t, 'seq', split_axis=0, concat_axis=1, tiled=True)]
  transfers between devices with their start and end apart: 4 -> 0, of which waited for: 3 -> 0; matrix products, arithmetic and copies ran while one was open for 13% -> 0% of each run, Pallas kernels for 0% -> 0%
where the time goes in v1:
time: 149 us; the launch traced here: 148 us
  Pallas kernels  136 us (91%)
  local copies, waits for them, and re-layouts  8.34 us (6%)
  other arithmetic  3.56 us (2%)
    pallas_call x1, Pallas kernels, local_fused(): pl.pallas_call(functools.partial(fused, ns, nch, lb, pp, width), out_shap...  136 us
    unnamed x9, local copies, waits for them, and re-layouts  6.02 us

profile of v1, /device:TPU:0, one launch (start us, length us, event | category | flops | bytes accessed | tf_op | source)
XLA Modules:
  0.0 148.3 jit_solution(1158433003674897324)
XLA Ops:
  0.6 135.7 %fused.1 = (bf16[8,8,2,64,128]{4,3,2,1,0:T(8,128)(2,1)}, bf16[8,8,2,64,128]{4,3,2,1,0:T(8,128)(2,1)}, bf16[8,8,2,64,128]{4,3,2,1,0:T(8,128)(2,1)}, bf16[2,512,1024]{2,1,0:T(8,128)(2,1)}, f32[64,128]{1,0:T(8,128)}) custom-call(bf16[8,8,2,64,128]{4,3,2,1,0:T(8,128)(2,1)} %bitcast.15, bf16[8,8,2,64,128]{4,3,2,1,0:T(8,128)(2,1)} %bitcast.16, ...), custom_call_target="tpu_custom_call" | custom-call | tf_op jit(solution)/shard_map/fused/pallas_call | solution.py:396
  136.3 1.4 slice_multiply_fusion
  137.7 2.2 %convert_multiply_fusion = f32[2,512,1024]{2,1,0:T(8,128)S(1)} fusion(bf16[2,512,1024]{2,1,0:T(8,128)(2,1)} %get-tuple-element.13), kind=kLoop, calls=%fused_computation | loop fusion | flops 2097152 | bytes 6291456 | tf_op jit(solution)/shard_map/div | solution.py:409
  139.9 0.0 copy-start.2
  139.9 2.3 %copy.10 = f32[8,2,64,1024]{3,2,1,0:T(8,128)} copy(f32[8,2,64,1024]{3,2,0,1:T(8,128)S(1)} %bitcast.10) | data formatting | bytes 8388608 | tf_op jit(solution)/shard_map/div | solution.py:409
  142.2 0.0 copy-done.2
  142.2 0.0 copy-start.1
  142.2 1.3 copy.14
  143.6 1.0 copy-done.1
  144.6 0.0 copy-start
  144.6 1.3 copy.15
  145.9 1.0 copy-done
  146.9 1.3 copy.16
Async XLA Ops:
  139.9 2.3 %copy-start.2 = (bf16[8,8,2,64,128]{4,3,2,1,0:T(8,128)(2,1)S(1)}, bf16[8,8,2,64,128]{4,3,2,1,0:T(8,128)(2,1)}, u32[]{:S(2)}) copy-start(bf16[8,8,2,64,128]{4,3,2,1,0:T(8,128)(2,1)} %get-tuple-element.10) | copy-start | bytes 6291460
  142.2 2.3 %copy-start.1 = (bf16[8,8,2,64,128]{4,3,2,1,0:T(8,128)(2,1)S(1)}, bf16[8,8,2,64,128]{4,3,2,1,0:T(8,128)(2,1)}, u32[]{:S(2)}) copy-start(bf16[8,8,2,64,128]{4,3,2,1,0:T(8,128)(2,1)} %get-tuple-element.11) | copy-start | bytes 6291460
  144.6 2.3 %copy-start = (bf16[8,8,2,64,128]{4,3,2,1,0:T(8,128)(2,1)S(1)}, bf16[8,8,2,64,128]{4,3,2,1,0:T(8,128)(2,1)}, u32[]{:S(2)}) copy-start(bf16[8,8,2,64,128]{4,3,2,1,0:T(8,128)(2,1)} %get-tuple-element.12) | copy-start | bytes 6291460

commit v2 on v1

--- a/solution.py
+++ b/solution.py
@@ -39,7 +39,7 @@
           mixed_hbm, gt_hbm, gg_hbm, gf_hbm, gs_ref,
           xv, gv, w1v, wk, wkt, act, fs, hid, dzt, ht, ght, ghr, mt, gfa, gtv,
           pf, pb, r1, s1b, r2, s2, s2b, r3, gfo, gsr, gsr2,
-          ld, dz_l, mx_l, out_l,
+          ld, dz_l, mx_l, out_l, gf_l,
           dz_s, dz_r, gh_s, gh_r, h_s, h_r, mx_s, mx_r,
           a1_s, a1_r, a2_s, a2_r, a3_s, a3_r, b3_s, b3_r, b2_s, b2_r, b1_s, b1_r,
           q_s, q_r, q2_s, q2_r):
@@ -258,15 +258,6 @@
     out_gt = pltpu.make_async_copy(gtv, gt_hbm, out_l.at[1])
     out_gt.start()
 
-    mx_own = [
-        pltpu.make_async_copy(mt.at[h, mine], mixed_hbm.at[:, me, h], mx_l.at[h]) for h in range(nc)
-    ]
-    for h in range(nc):
-        recv(h_copy, h, ns)
-        mix(wk, ht, mt, h)
-        start(mx_copy, h, ns)
-        mx_own[h].start()
-
     for h in range(nc):
         recv(a2, h, nch)
         low = pl.multiple_of(core * half + zz * zrows, zrows)
@@ -276,6 +267,28 @@
         s2[h] = total
         s2b[h] = total.astype(BF)
         start(a3, h, nq)
+
+    for h in range(nc):
+        recv(a3, h, nq)
+        total = s2[h, pl.ds(pl.multiple_of(quad * qrows, qrows), qrows), :]
+        for d in range(1, nq):
+            total = total + r3[h, d].astype(F32)
+        gfo[h, pl.ds(pl.multiple_of(core * half + zz * zrows + quad * qrows, qrows), qrows), :] = total.astype(BF)
+        start(b3, h, nq)
+
+    mx_own = [
+        pltpu.make_async_copy(mt.at[h, mine], mixed_hbm.at[:, me, h], mx_l.at[h]) for h in range(nc)
+    ]
+    for h in range(nc):
+        if h == nc - 1:
+            for e in range(nc):
+                recv(b3, e, nq)
+                sent(b3, e, nq)
+                start(b2, e, nch)
+        recv(h_copy, h, ns)
+        mix(wk, ht, mt, h)
+        start(mx_copy, h, ns)
+        mx_own[h].start()
 
     def second(t):
         rows = pl.ds(t * (tile // GRP), tile // GRP)
@@ -301,19 +314,6 @@
 
     start(q1, 0, ns)
 
-    for h in range(nc):
-        recv(a3, h, nq)
-        total = s2[h, pl.ds(pl.multiple_of(quad * qrows, qrows), qrows), :]
-        for d in range(1, nq):
-            total = total + r3[h, d].astype(F32)
-        gfo[h, pl.ds(pl.multiple_of(core * half + zz * zrows + quad * qrows, qrows), qrows), :] = total.astype(BF)
-        start(b3, h, nq)
-
-    for h in range(nc):
-        recv(b3, h, nq)
-        sent(b3, h, nq)
-        start(b2, h, nch)
-
     recv(q1, 0, ns)
     sent(q1, 0, ns)
     total = gsr[0]
@@ -332,13 +332,17 @@
     total = gsr2[0]
     for d in range(1, nch):
         total = total + gsr2[d]
-    gs_ref[...] = total
+    gs_ref[...] = total[:, :nb] / jnp.sqrt(F32(block * width * nch))
 
     for h in range(nc):
         b1(h).wait_recv()
         b1(h).wait_send()
-    out_gf = pltpu.make_async_copy(gfo, gf_hbm, out_l.at[2])
-    out_gf.start()
+    def out_gf(h, p):
+        rows = pl.ds(pl.multiple_of(p * pc, pc), pc)
+        return pltpu.make_async_copy(gfo.at[h, rows], gf_hbm.at[p, h], gf_l.at[h, p])
+
+    for h in range(nc):
+        loop(0, ns, lambda p: out_gf(h, p).start())
 
     for h in range(nc):
         sent(dz_copy, h, ns)
@@ -353,7 +357,16 @@
         sent(mx_copy, h, ns)
     out_gg.wait()
     out_gt.wait()
-    out_gf.wait()
+    for h in range(nc):
+        loop(0, ns, lambda p: out_gf(h, p).wait())
+
+
+def finish(terms, mixed, gt, gg, gf, gs, mixed_out, gt_out, gg_out, gf_out, gs_out):
+    mixed_out[...] = mixed[...]
+    gt_out[...] = gt[...]
+    gg_out[...] = gg[...]
+    gf_out[...] = gf[...].astype(F32) / jnp.sqrt(F32(terms))
+    gs_out[...] = gs[...]
 
 
 def local_fused(tokens, gate, cotangent, w_first, w_second):
@@ -387,7 +400,7 @@
         V((nc, nch, zrows, block), BF), V((nc, zrows, block), F32), V((nc, zrows, block), BF),
         V((nc, nq, qrows, block), BF), V((nc, 2 * half, block), BF),
         V((ns, nb, 128), F32), V((nch, nb, 128), F32),
-        D((3,)), D((nc,)), D((nc,)), D((3,)),
+        D((3,)), D((nc,)), D((nc,)), D((2,)), D((nc, ns)),
     ]
     scratch += [D((nc, ns))] * 8
     scratch += [D((nc,))] * 2 + [D((nc, nch))] * 2 + [D((nc, nq))] * 4 + [D((nc, nch))] * 2 + [D((nc,))] * 2
@@ -395,7 +408,7 @@
     sd = jax.ShapeDtypeStruct
     mixed, gt, gg, gf, gs = pl.pallas_call(
         functools.partial(fused, ns, nch, lb, pp, width),
-        out_shape=(sd(five, BF), sd(five, BF), sd(five, BF), sd((nc, 2 * half, block), BF), sd((nb, 128), F32)),
+        out_shape=(sd(five, BF), sd(five, BF), sd(five, BF), sd((ns, nc, pc, block), BF), sd((nb, nb), F32)),
         in_specs=[anyspec] * 4 + [vmem],
         out_specs=(anyspec, anyspec, anyspec, anyspec, vmem),
         scratch_shapes=scratch,
@@ -405,10 +418,15 @@
         name="fused",
     )(tokens.reshape(five), gate.reshape(five), cotangent.reshape(five), w_first, w_second)
     total_width = width * nch
-    gf = gf.reshape(nc, ns, pc, block).transpose(1, 0, 2, 3).reshape(block, block)
-    grad_first = gf.astype(F32) / jnp.sqrt(F32(nb * total_width))
-    grad_second = gs[:, :nb] / jnp.sqrt(F32(block * total_width))
-    return mixed.reshape(tokens.shape), gt.reshape(tokens.shape), gg.reshape(tokens.shape), grad_first, grad_second
+    rows, cells = pl.BlockSpec((block, width), lambda i: (i, 0)), pl.BlockSpec((block // lb, block), lambda i: (i, 0))
+    return pl.pallas_call(
+        functools.partial(finish, nb * width * nch),
+        grid=(lb,),
+        out_shape=(sd(tokens.shape, BF),) * 3 + (sd((block, block), F32), sd((nb, nb), F32)),
+        in_specs=[rows] * 3 + [cells, vmem],
+        out_specs=(rows, rows, rows, cells, pl.BlockSpec((nb, nb), lambda i: (0, 0))),
+        name="finish",
+    )(mixed.reshape(tokens.shape), gt.reshape(tokens.shape), gg.reshape(tokens.shape), gf.reshape(block, block), gs)
 
 
 def local(tokens, gate, cotangent, w_first, w_second):
@@ -468,7 +486,7 @@
     pp = block // ns
     if width != 128 or lb % 2 or ns % 2 or lb * ns * GRP > 1024 or (lb * ns * GRP) % 256:
         return False
-    if block > 1024 or block % 256 or 256 % pp or pp % (CHUNKS * 2 * GRP):
+    if block > 1024 or block % 256 or block % (lb * GRP) or 256 % pp or pp % (CHUNKS * 2 * GRP):
         return False
     return (block // CHUNKS) % (ns * nch * GRP) == 0 and lb * ns <= 128 and lb <= 8
 

time: 149 us -> 129 us (0.87)
  local copies, waits for them, and re-layouts: 8.34 us -> 0 us
  Pallas kernels: 136 us -> 128 us
  other arithmetic: 3.56 us -> 0 us
    pallas_call x1, Pallas kernels: 136 us -> 118 us  [local_fused(): pl.pallas_call(functools.partial(fused, ns, nch, lb, pp, width), out_shap...]
    pallas_call x0 -> x1, Pallas kernels: none -> 9.28 us  [local_fused(): pl.pallas_call(functools.partial(finish, nb * width * nch), grid=(lb,), o...]
    unnamed x9 -> x0, local copies, waits for them, and re-layouts: 6.02 us -> none
    div x2 -> x0, other arithmetic: 3.56 us -> none  [the longest x1 2.18 us: local_fused(): grad_first = gf.astype(F32) / jnp.sqrt(F32(nb * total_width))]
    div x1 -> x0, local copies, waits for them, and re-layouts: 2.32 us -> none  [local_fused(): grad_first = gf.astype(F32) / jnp.sqrt(F32(nb * total_width))]
where the time goes in v2:
time: 129 us; the launch traced here: 128 us
  Pallas kernels  128 us (99%)
    pallas_call x1, Pallas kernels, local_fused(): pl.pallas_call(functools.partial(fused, ns, nch, lb, pp, width), out_shap...  118 us
    pallas_call x1, Pallas kernels, local_fused(): pl.pallas_call(functools.partial(finish, nb * width * nch), grid=(lb,), o...  9.28 us

profile of v2, /device:TPU:0, one launch (start us, length us, event | category | flops | bytes accessed | tf_op | source)
XLA Modules:
  0.0 128.3 jit_solution(14432240033011836942)
XLA Ops:
  0.6 118.4 %fused.1 = (bf16[8,8,2,64,128]{4,3,2,1,0:T(8,128)(2,1)}, bf16[8,8,2,64,128]{4,3,2,1,0:T(8,128)(2,1)}, bf16[8,8,2,64,128]{4,3,2,1,0:T(8,128)(2,1)}, bf16[8,2,64,1024]{3,2,1,0:T(8,128)(2,1)}, f32[64,64]{1,0:T(8,128)}) custom-call(bf16[8,8,2,64,128]{4,3,2,1,0:T(8,128)(2,1)} %bitcast.7, bf16[8,8,2,64,128]{4,3,2,1,0:T(8,128)(2,1)} %bitcast.8, ...), custom_call_target="tpu_custom_call" | custom-call | tf_op jit(solution)/shard_map/fused/pallas_call | solution.py:409
  119.0 9.3 %finish.1 = (bf16[8192,128]{1,0:T(8,128)(2,1)}, bf16[8192,128]{1,0:T(8,128)(2,1)}, bf16[8192,128]{1,0:T(8,128)(2,1)}, f32[1024,1024]{1,0:T(8,128)}, f32[64,64]{1,0:T(8,128)}) custom-call(bf16[8192,128]{1,0:T(8,128)(2,1)} %bitcast.10, bf16[8192,128]{1,0:T(8,128)(2,1)} %bitcast.11, bf16[8192,128]{1,0:T(8,128)(2,1)} %bitcast.12, bf16[1024,1024]{1,0:T(8,128)(2,1)} %bitcast.13, ...), custom_call_target="tpu_custom_call" | custom-call | tf_op jit(solution)/shard_map/finish/pallas_call | solution.py:422
